TPU v7x, 128 devices: a whole 4x4x4 slice. The times are simulated.
128 devices in a mesh: shard: 4 (over y_lo, core), rep: 32 (over x, y_hi, z).
Axes of the slice: x: 4, y: 4 (y_hi: 2, y_lo: 2; y = y_hi * 2 + y_lo), z: 4, core: 2. Of those that a mesh axis runs over, the one named last changes fastest.
Arguments:
- tokens: bfloat16 [32, 512, 768], P('rep', 'shard'), may hold values from -6 to 6
- lengths: int32 [32, 4], P('rep'), may hold values from 1 to 509, as said below
- routes: int32 [32, 512], P('rep', 'shard'), may hold values from 0 to 3, as said below
- attn_in: bfloat16 [2, 768, 2304], P(None, 'shard'), may hold values from -0.21875 to 0.21875
- attn_proj: bfloat16 [2, 768, 768], P(None, 'shard'), may hold values from -0.875 to 0.875
- norm_first: float32 [2, 768], replicated, may hold values from 0.5 to 1.5
- norm_second: float32 [2, 768], replicated, may hold values from 0.5 to 1.5
- rel_bias: float32 [2, 32, 12], replicated, may hold values from -4 to 4
- router: bfloat16 [2, 768, 4], replicated, may hold values from -0.15625 to 0.15625
- expert_in: bfloat16 [2, 4, 768, 3072], P(None, 'shard'), may hold values from -0.21875 to 0.21875
- expert_out: bfloat16 [2, 4, 3072, 768], P(None, 'shard'), may hold values from -0.4375 to 0.4375
- cotangent: bfloat16 [32, 512, 768], P('rep', 'shard'), may hold values from -6 to 6
Outputs:
- result: bfloat16 [32, 512, 768], P('rep', 'shard')
- tokens_grad: bfloat16 [32, 512, 768], P('rep', 'shard')
- attn_in_grad: float32 [2, 768, 2304], P(None, ('shard', 'rep'))
- attn_proj_grad: float32 [2, 768, 768], P(None, ('shard', 'rep'))
- norm_first_grad: float32 [2, 768], P(None, ('shard', 'rep'))
- norm_second_grad: float32 [2, 768], P(None, ('shard', 'rep'))
- rel_bias_grad: float32 [2, 384], P(None, ('shard', 'rep'))
- router_grad: float32 [2, 768, 4], P(None, ('shard', 'rep'))
- expert_in_grad: float32 [2, 4, 768, 3072], P(None, 'shard', 'rep')
- expert_out_grad: float32 [2, 4, 3072, 768], P(None, 'shard', 'rep')
Inputs may be any that keep to these rules, and one draw needn't show every extreme that they name: Each group's 4 lengths are positive and sum to 512; one of them exceeds 512 - 128. `routes`: among the 128 tokens of one device at most 64 name one expert; in each group one expert is named by exactly 64 tokens of every device of the group.
All inputs are finite; a program needn't handle non-finite values.
Results may differ from a plain program's by a relative error of at most 0.033.
Values may be sent and summed in bfloat16 or wider, within the bound.
No kernel may reach another device: no remote copies, remote signals or barrier semaphores. Data moves between devices by JAX's collectives and lax.ppermute only.
A program may use at most 256 MiB of HBM per device.

v0:
```python
import jax
import jax.numpy as jnp
from jax import lax
from jax.sharding import PartitionSpec as P

EPS = 1e-06
SCALE = 0.125
NEG = -1e30
THRESHOLDS = (12, 16, 23, 32, 46, 64, 91)
HIGH = lax.Precision.HIGHEST


def bucket_of(offset):
    distance = jnp.abs(offset)
    far_bucket = 8 + sum(((distance >= threshold).astype(jnp.int32) for threshold in THRESHOLDS))
    bucket_id = jnp.where(distance < 8, distance, far_bucket)
    return bucket_id + 16 * (offset > 0).astype(jnp.int32)


def rms_norm(vector, gain_vec):
    return vector * lax.rsqrt(jnp.mean(vector * vector, -1, keepdims=True) + EPS) * gain_vec


def norm_back(vector, gain_vec, upstream):
    inverse = lax.rsqrt(jnp.mean(vector * vector, -1, keepdims=True) + EPS)
    scaled = upstream * gain_vec
    grad_gain = jnp.sum(upstream * vector * inverse, 0)
    grad_in = inverse * scaled - vector * (inverse * inverse * inverse) * jnp.mean(
        scaled * vector, -1, keepdims=True
    )
    return (grad_in, grad_gain)


def gelu_tanh(vector):
    return jax.nn.gelu(vector, approximate=True)


def dispatch_table(route_rows, experts, capacity):
    onehot = (route_rows[..., None] == jnp.arange(experts, dtype=jnp.int32)).astype(jnp.int32)
    position = jnp.sum(jnp.cumsum(onehot, axis=-2) * onehot, -1) - 1
    target = route_rows * capacity + position
    return (
        jnp.arange(experts * capacity, dtype=jnp.int32)[:, None] == target[..., None, :]
    ).astype(jnp.float32)


def on_device(
    tokens,
    lengths,
    routes,
    attn_in,
    attn_proj,
    norm_first,
    norm_second,
    rel_bias,
    router,
    expert_in,
    expert_out,
    cotangent,
):
    shard_pos = lax.axis_index("shard")
    shard_count = lax.axis_size("shard")
    x_rows = tokens[0].astype(jnp.float32)
    per_device, model_width = x_rows.shape
    group_tok = per_device * shard_count
    bucket_count = rel_bias.shape[1]
    head_count = rel_bias.shape[2]
    head_size = model_width // head_count
    experts = router.shape[2]
    capacity = per_device // 2
    levels = attn_in.shape[0]
    query_pos = shard_pos * per_device + jnp.arange(per_device, dtype=jnp.int32)
    key_pos = jnp.arange(group_tok, dtype=jnp.int32)
    bucket_hot = (
        bucket_of(key_pos[None, :] - query_pos[:, None])[..., None]
        == jnp.arange(bucket_count, dtype=jnp.int32)
    ).astype(jnp.float32)
    ends = jnp.cumsum(lengths[0])
    doc_query = jnp.sum((query_pos[:, None] >= ends[None, :]).astype(jnp.int32), -1)
    doc_key = jnp.sum((key_pos[:, None] >= ends[None, :]).astype(jnp.int32), -1)
    same_doc = doc_query[:, None] == doc_key[None, :]
    route_row = routes[0]
    dispatch = dispatch_table(route_row, experts, capacity).astype(jnp.bfloat16)
    collect = dispatch.T
    chosen = (route_row[:, None] == jnp.arange(experts, dtype=jnp.int32)).astype(jnp.float32)

    def scores_of(query_part, key_all, bias_rows):
        rel_terms = jnp.einsum("ijb,bh->hij", bucket_hot, bias_rows, precision=HIGH)
        raw = (
            jnp.einsum("ihd,jhd->hij", query_part, key_all, preferred_element_type=jnp.float32)
            * SCALE
            + rel_terms
        )
        return jnp.where(same_doc[None], raw, NEG)

    saved = []
    stream = x_rows
    for level in range(levels):
        w_qkv, w_proj = (
            lax.all_gather(attn_in[level], "shard", axis=0, tiled=True),
            lax.all_gather(attn_proj[level], "shard", axis=0, tiled=True),
        )
        normed = rms_norm(stream, norm_first[level]).astype(jnp.bfloat16)
        proj_qkv = jnp.dot(normed, w_qkv, preferred_element_type=jnp.float32).astype(jnp.bfloat16)
        query_part = proj_qkv[:, :model_width].reshape(per_device, head_count, head_size)
        key_value = lax.all_gather(proj_qkv[:, model_width:], "shard", axis=0, tiled=True)
        key_all = key_value[:, :model_width].reshape(group_tok, head_count, head_size)
        value_all = key_value[:, model_width:].reshape(group_tok, head_count, head_size)
        scores = scores_of(query_part, key_all, rel_bias[level])
        top_score = jnp.max(scores, -1, keepdims=True)
        expo = jnp.exp(scores - top_score)
        total = jnp.sum(expo, -1, keepdims=True)
        attn_probs = (expo / total).astype(jnp.bfloat16)
        log_total = top_score + jnp.log(total)
        attn_mixed = jnp.einsum(
            "hij,jhd->ihd", attn_probs, value_all, preferred_element_type=jnp.float32
        )
        attn_mixed = attn_mixed.reshape(per_device, model_width).astype(jnp.bfloat16)
        after_attn = stream + jnp.dot(attn_mixed, w_proj, preferred_element_type=jnp.float32)
        normed_two = rms_norm(after_attn, norm_second[level]).astype(jnp.bfloat16)
        logits = jnp.dot(normed_two, router[level], preferred_element_type=jnp.float32)
        route_probs = jax.nn.softmax(logits, -1)
        gate_value = jnp.sum(route_probs * chosen, -1)
        slot_rows = jnp.dot(dispatch, normed_two, preferred_element_type=jnp.float32).astype(
            jnp.bfloat16
        )
        slot_rows = slot_rows.reshape(experts, capacity, model_width)
        w_inner = expert_in[level, 0]
        w_outer = expert_out[level, 0]
        arrived_rows = lax.all_to_all(slot_rows, "shard", split_axis=0, concat_axis=0, tiled=True)
        hidden_part = jnp.einsum(
            "skd,df->skf", arrived_rows, w_inner, preferred_element_type=jnp.float32
        )
        active_part = gelu_tanh(hidden_part).astype(jnp.bfloat16)
        produced = jnp.einsum(
            "skf,fd->skd", active_part, w_outer, preferred_element_type=jnp.float32
        ).astype(jnp.bfloat16)
        came_back = lax.all_to_all(produced, "shard", split_axis=0, concat_axis=0, tiled=True)
        arrived = arrived_rows
        hidden = hidden_part
        combined = jnp.dot(
            collect,
            came_back.reshape(experts * capacity, model_width),
            preferred_element_type=jnp.float32,
        )
        stream_next = after_attn + gate_value[:, None] * combined
        saved.append(
            (
                stream,
                normed,
                query_part,
                key_all,
                value_all,
                attn_probs,
                log_total,
                attn_mixed,
                after_attn,
                normed_two,
                route_probs,
                gate_value,
                combined,
                arrived,
                hidden,
                w_qkv,
                w_proj,
            )
        )
        stream = stream_next
    result = stream.astype(jnp.bfloat16)[None]
    upstream = cotangent[0].astype(jnp.float32)
    list_qkv, list_proj, list_first, list_second, list_bias, list_router, list_inner, list_outer = (
        [],
        [],
        [],
        [],
        [],
        [],
        [],
        [],
    )
    for level in reversed(range(levels)):
        (
            stream_in,
            normed,
            query_part,
            key_all,
            value_all,
            attn_probs,
            log_total,
            attn_mixed,
            after_attn,
            normed_two,
            route_probs,
            gate_value,
            combined,
            arrived,
            hidden,
            kept_qkv,
            kept_proj,
        ) = saved[level]
        w_qkv, w_proj = (
            lax.all_gather(attn_in[level], "shard", axis=0, tiled=True),
            lax.all_gather(attn_proj[level], "shard", axis=0, tiled=True),
        )
        w_inner = expert_in[level, 0]
        w_outer = expert_out[level, 0]
        grad_gate = jnp.sum(upstream * combined, -1)
        to_send = (gate_value[:, None] * upstream).astype(jnp.bfloat16)
        slot_grads = jnp.dot(dispatch, to_send, preferred_element_type=jnp.float32).astype(
            jnp.bfloat16
        )
        slot_grads = slot_grads.reshape(experts, capacity, model_width)
        arrived_grad = lax.all_to_all(slot_grads, "shard", split_axis=0, concat_axis=0, tiled=True)
        active_grad = jnp.einsum(
            "skd,fd->skf", arrived_grad, w_outer, preferred_element_type=jnp.float32
        )
        active = gelu_tanh(hidden).astype(jnp.bfloat16)
        _, gelu_pull = jax.vjp(gelu_tanh, hidden)
        hidden_grad = gelu_pull(active_grad)[0].astype(jnp.bfloat16)
        grad_outer = jnp.einsum(
            "skf,skd->fd", active, arrived_grad, preferred_element_type=jnp.float32
        )
        grad_inner = jnp.einsum(
            "skd,skf->df", arrived, hidden_grad, preferred_element_type=jnp.float32
        )
        rows_grad = jnp.einsum(
            "skf,df->skd", hidden_grad, w_inner, preferred_element_type=jnp.float32
        ).astype(jnp.bfloat16)
        slot_back = lax.all_to_all(rows_grad, "shard", split_axis=0, concat_axis=0, tiled=True)
        normed_grad = jnp.dot(
            collect,
            slot_back.reshape(experts * capacity, model_width),
            preferred_element_type=jnp.float32,
        )
        logit_grad = grad_gate[:, None] * gate_value[:, None] * (chosen - route_probs)
        normed_grad = normed_grad + jnp.dot(
            logit_grad, router[level].astype(jnp.float32).T, precision=HIGH
        )
        grad_router = jnp.dot(normed_two.astype(jnp.float32).T, logit_grad, precision=HIGH)
        attn_side, grad_second = norm_back(after_attn, norm_second[level], normed_grad)
        after_grad = upstream + attn_side
        branch_grad = after_grad.astype(jnp.bfloat16)
        grad_proj = jnp.dot(attn_mixed.T, branch_grad, preferred_element_type=jnp.float32)
        mixed_grad = jnp.dot(branch_grad, w_proj.T, preferred_element_type=jnp.float32).astype(
            jnp.bfloat16
        )
        mixed_grad = mixed_grad.reshape(per_device, head_count, head_size)
        scores = scores_of(query_part, key_all, rel_bias[level])
        full_probs = jnp.exp(scores - log_total)
        probs_grad = jnp.einsum(
            "ihd,jhd->hij", mixed_grad, value_all, preferred_element_type=jnp.float32
        )
        score_grad = full_probs * (probs_grad - jnp.sum(full_probs * probs_grad, -1, keepdims=True))
        score_grad = score_grad.astype(jnp.bfloat16)
        grad_bias = jnp.einsum(
            "hij,ijb->bh", score_grad.astype(jnp.float32), bucket_hot, precision=HIGH
        )
        query_grad = (
            jnp.einsum("hij,jhd->ihd", score_grad, key_all, preferred_element_type=jnp.float32)
            * SCALE
        )
        key_grad = (
            jnp.einsum("hij,ihd->jhd", score_grad, query_part, preferred_element_type=jnp.float32)
            * SCALE
        )
        value_grad = jnp.einsum(
            "hij,ihd->jhd", attn_probs, mixed_grad, preferred_element_type=jnp.float32
        )
        pair_grad = jnp.concatenate(
            [key_grad.reshape(group_tok, model_width), value_grad.reshape(group_tok, model_width)],
            1,
        )
        own_pair = lax.psum_scatter(pair_grad, "shard", scatter_dimension=0, tiled=True)
        qkv_grad = jnp.concatenate(
            [query_grad.reshape(per_device, model_width), own_pair], 1
        ).astype(jnp.bfloat16)
        grad_qkv = jnp.dot(normed.T, qkv_grad, preferred_element_type=jnp.float32)
        first_grad = jnp.dot(qkv_grad, w_qkv.T, preferred_element_type=jnp.float32)
        input_side, grad_first = norm_back(stream_in, norm_first[level], first_grad)
        upstream = after_grad + input_side
        list_qkv.append(grad_qkv)
        list_proj.append(grad_proj)
        list_first.append(grad_first)
        list_second.append(grad_second)
        list_bias.append(grad_bias.reshape(-1))
        list_router.append(grad_router)
        list_inner.append(grad_inner)
        list_outer.append(grad_outer)

    def stacked(items):
        return jnp.stack(items[::-1], 0)

    attn_in_grad, attn_proj_grad, norm_first_grad, norm_second_grad, rel_bias_grad, router_grad = (
        lax.psum_scatter(stacked(list_qkv), ("shard", "rep"), scatter_dimension=1, tiled=True),
        lax.psum_scatter(stacked(list_proj), ("shard", "rep"), scatter_dimension=1, tiled=True),
        lax.psum_scatter(stacked(list_first), ("shard", "rep"), scatter_dimension=1, tiled=True),
        lax.psum_scatter(stacked(list_second), ("shard", "rep"), scatter_dimension=1, tiled=True),
        lax.psum_scatter(stacked(list_bias), ("shard", "rep"), scatter_dimension=1, tiled=True),
        lax.psum_scatter(stacked(list_router), ("shard", "rep"), scatter_dimension=1, tiled=True),
    )
    expert_in_grad, expert_out_grad = (
        lax.psum_scatter(stacked(list_inner)[:, None], "rep", scatter_dimension=2, tiled=True),
        lax.psum_scatter(stacked(list_outer)[:, None], "rep", scatter_dimension=2, tiled=True),
    )
    tokens_grad = upstream.astype(jnp.bfloat16)[None]
    return (
        result,
        tokens_grad,
        attn_in_grad,
        attn_proj_grad,
        norm_first_grad,
        norm_second_grad,
        rel_bias_grad,
        router_grad,
        expert_in_grad,
        expert_out_grad,
    )


def solution(mesh):
    return jax.shard_map(
        on_device,
        mesh=mesh,
        in_specs=(
            P("rep", "shard", None),
            P("rep", None),
            P("rep", "shard"),
            P(None, "shard", None),
            P(None, "shard", None),
            P(),
            P(),
            P(),
            P(),
            P(None, "shard", None, None),
            P(None, "shard", None, None),
            P("rep", "shard", None),
        ),
        out_specs=(
            P("rep", "shard", None),
            P("rep", "shard", None),
            P(None, ("shard", "rep"), None),
            P(None, ("shard", "rep"), None),
            P(None, ("shard", "rep")),
            P(None, ("shard", "rep")),
            P(None, ("shard", "rep")),
            P(None, ("shard", "rep"), None),
            P(None, "shard", "rep", None),
            P(None, "shard", "rep", None),
        ),
        check_vma=False,
    )
```

profile of v0, /device:TPU:0, one launch (start us, length us, event | category | flops | bytes accessed | tf_op | source)
XLA Modules:
  0.0 1261.6 jit_solution(17418359552196407631)
XLA Ops:
  10.8 42.5 %all-gather.15.cloned.1.call-done = bf16[1,768,2304]{2,1,0:T(8,128)(2,1)} async-done(((bf16[1,192,2304]{2,1,0:T(8,128)(2,1)}), bf16[1,768,2304]{2,1,0:T(8,128)(2,1)}) %all-gather.15.cloned.1.call-update) | async-done | bytes 3538960 | tf_op jit(solution)/shard_map/all_gather | solution.py:100
  66.4 16.7 %all-gather.11.cloned.1.call-done = bf16[512,1536]{1,0:T(8,128)(2,1)} async-done(((bf16[128,1536]{1,0:T(8,128)(2,1)}), bf16[512,1536]{1,0:T(8,128)(2,1)}) %all-gather.11.cloned.1.call-update) | async-done | bytes 1572880 | tf_op jit(solution)/shard_map/all_gather | solution.py:106
  95.3 12.6 all-gather.17.cloned.1.call-done
  118.9 6.7 all-to-all-done
  131.2 5.1 fusion.68
  142.6 9.2 all-to-all-done.1
  162.0 5.1 fusion.2
  170.4 16.8 %all-gather.13.cloned.1.call-done = bf16[512,1536]{1,0:T(8,128)(2,1)} async-done(((bf16[128,1536]{1,0:T(8,128)(2,1)}), bf16[512,1536]{1,0:T(8,128)(2,1)}) %all-gather.13.cloned.1.call-update) | async-done | bytes 1572880 | tf_op jit(solution)/shard_map/all_gather | solution.py:106
  203.7 7.6 all-gather.21.cloned.1.call-done
  249.2 6.1 fusion.51
  293.9 34.9 %reduce-scatter.9.cloned.1.call-done = f32[128,1536]{0,1:T(8,128)} async-done(((f32[512,1536]{0,1:T(8,128)}), f32[128,1536]{0,1:T(8,128)}) %reduce-scatter.9.cloned.1.call-update) | async-done | bytes 786448 | tf_op jit(solution)/shard_map/reduce_scatter | solution.py:273
  336.2 10.0 all_to_all.40
  346.2 5.3 fusion.44
  361.0 5.5 all-to-all-done.7
  388.8 5.8 copy.109
  395.3 25.1 %reduce-scatter.11.cloned.1.call-done = f32[128,1536]{0,1:T(8,128)} async-done(((f32[512,1536]{0,1:T(8,128)}), f32[128,1536]{0,1:T(8,128)}) %reduce-scatter.11.cloned.1.call-update) | async-done | bytes 786448 | tf_op jit(solution)/shard_map/reduce_scatter | solution.py:273
  426.4 11.0 pad_maximum_fusion
  437.3 26.8 %copy.108 = f32[2,768,2304]{2,0,1:T(2,128)} copy(f32[2,768,2304]{2,1,0:T(8,128)} %pad_maximum_fusion) | data formatting | bytes 28311552 | tf_op jit(solution)/shard_map/stack | solution.py:291
  471.0 7.1 maximum_bitcast_fusion.1
  484.6 7.1 maximum_bitcast_fusion
  507.7 67.7 %all-reduce.6 = (f32[2,768]{1,0:T(2,128)S(1)}, f32[2,768]{1,0:T(2,128)S(1)}, f32[2,384]{1,0:T(2,128)S(1)}, f32[2,768,4]{1,2,0:T(4,128)S(1)}) all-reduce(f32[2,768]{1,0:T(2,128)S(1)} %pad_maximum_fusion.11, f32[2,768]{1,0:T(2,128)S(1)} %pad_maximum_fusion.12, ...), channel_id=10, replica_groups=mesh['shard'=4,'rep'=32] {'shard','rep'}, use_global_device_ids=true, to_apply=%region_33.34.clone | all-reduce | flops 9984 | bytes 79872
  578.2 109.1 %all-reduce.10.cloned.1.call-done = (f32[2,768,2304]{2,0,1:T(2,128)}, f32[2,768,768]{2,0,1:T(2,128)}) async-done(((f32[2,768,2304]{2,0,1:T(2,128)}, f32[2,768,768]{2,0,1:T(2,128)}), (f32[2,768,2304]{2,0,1:T(2,128)}, f32[2,768,768]{2,0,1:T(2,128)})) %all-reduce.10.cloned.1.call-update) | async-done | bytes 18874384
  690.2 281.7 %reduce-scatter.15.cloned.1.call-done = f32[2,1,96,768]{3,2,0,1:T(8,128)} async-done(((f32[2,1,3072,768]{3,2,0,1:T(8,128)}), f32[2,1,96,768]{3,2,0,1:T(8,128)}) %reduce-scatter.15.cloned.1.call-update) | async-done | bytes 589840 | tf_op jit(solution)/shard_map/reduce_scatter | solution.py:303
  971.9 282.7 %reduce-scatter.13.cloned.1.call-done = f32[2,1,24,3072]{3,2,0,1:T(8,128)} async-done(((f32[2,1,768,3072]{3,2,0,1:T(8,128)}), f32[2,1,24,3072]{3,2,0,1:T(8,128)}) %reduce-scatter.13.cloned.1.call-update) | async-done | bytes 589840 | tf_op jit(solution)/shard_map/reduce_scatter | solution.py:302
  (341 shorter events, 238.1 us)
Async XLA Ops:
  7.2 46.2 %all-gather.15.cloned.1.call-start = ((), (), s32[]{:S(2)}) async-start(), calls=%async_computation.18 | async-start | bytes 4423680 | tf_op jit(solution)/shard_map/all_gather | solution.py:100
  10.1 46.9 %copy-start.47 = (bf16[2,192,768]{2,1,0:T(8,128)(2,1)S(1)}, bf16[2,192,768]{2,1,0:T(8,128)(2,1)}, u32[]{:S(2)}) copy-start(bf16[2,192,768]{2,1,0:T(8,128)(2,1)} %param.16) | copy-start | bytes 1769476
  10.1 73.0 %all-gather.11.cloned.1.call-start = ((), (), s32[]{:S(2)}) async-start(), calls=%async_computation.12 | async-start | bytes 1966080 | tf_op jit(solution)/shard_map/all_gather | solution.py:106
  10.8 47.0 %copy-start.64 = (f32[128]{0:T(128)}, f32[128]{0:T(128)S(1)}, u32[]{:S(2)}) copy-start(f32[128]{0:T(128)S(1)} %get-tuple-element.89) | copy-start | bytes 1540
  56.9 51.0 %all-gather.17.cloned.1.call-start = ((), (), s32[]{:S(2)}) async-start(), calls=%async_computation.19 | async-start | bytes 1474560 | tf_op jit(solution)/shard_map/all_gather | solution.py:101
  57.8 99.2 %all-gather.19.cloned.1.call-start = ((), (), s32[]{:S(2)}) async-start(), calls=%async_computation.20 | async-start | bytes 4423680 | tf_op jit(solution)/shard_map/all_gather | solution.py:100
  95.3 34.2 %copy-start.32 = (bf16[12,64,128]{2,1,0:T(8,128)(2,1)}, bf16[12,64,128]{2,1,0:T(8,128)(2,1)S(1)}, u32[]{:S(2)}) copy-start(bf16[12,64,128]{2,1,0:T(8,128)(2,1)S(1)} %convolution_convert_fusion.7) | copy-start | bytes 589828
  112.8 12.8 %all-to-all-start = ((bf16[4,64,768]{2,1,0:T(8,128)(2,1)}), bf16[4,64,768]{2,1,0:T(8,128)(2,1)}, u32[]{:S(2)}, u32[]{:S(2)}) async-start(bf16[4,64,768]{2,1,0:T(8,128)(2,1)} %bitcast.301), calls=%async_computation | async-start | bytes 786432 | tf_op jit(solution)/shard_map/all_to_all | solution.py:130
  136.3 15.4 %all-to-all-start.1 = ((bf16[4,64,768]{2,1,0:T(8,128)(2,1)}), bf16[4,64,768]{2,1,0:T(8,128)(2,1)S(1)}, u32[]{:S(2)}, u32[]{:S(2)}) async-start(bf16[4,64,768]{2,1,0:T(8,128)(2,1)} %fusion.68), calls=%async_computation.1 | async-start | bytes 786432 | tf_op jit(solution)/shard_map/all_to_all | solution.py:138
  139.8 47.5 %all-gather.13.cloned.1.call-start = ((), (), s32[]{:S(2)}) async-start(), calls=%async_computation.13 | async-start | bytes 1966080 | tf_op jit(solution)/shard_map/all_gather | solution.py:106
  161.4 50.0 %all-gather.21.cloned.1.call-start = ((), (), s32[]{:S(2)}) async-start(), calls=%async_computation.21 | async-start | bytes 1474560 | tf_op jit(solution)/shard_map/all_gather | solution.py:101
  218.3 11.6 all-to-all-start.2
  230.0 14.7 %all-to-all-start.4 = ((bf16[4,64,768]{2,1,0:T(8,128)(2,1)}), bf16[4,64,768]{2,1,0:T(8,128)(2,1)}, u32[]{:S(2)}, u32[]{:S(2)}) async-start(bf16[4,64,768]{2,1,0:T(8,128)(2,1)} %bitcast.297), calls=%async_computation.4 | async-start | bytes 786432 | tf_op jit(solution)/shard_map/all_to_all | solution.py:213
  244.6 16.3 %all-to-all-start.3 = ((bf16[4,64,768]{2,1,0:T(8,128)(2,1)}), bf16[4,64,768]{2,1,0:T(8,128)(2,1)}, u32[]{:S(2)}, u32[]{:S(2)}) async-start(bf16[4,64,768]{2,1,0:T(8,128)(2,1)} %fusion.62), calls=%async_computation.3 | async-start | bytes 786432 | tf_op jit(solution)/shard_map/all_to_all | solution.py:138
  260.9 11.6 all-to-all-start.5
  265.0 63.8 %reduce-scatter.9.cloned.1.call-start = ((), (), s32[]{:S(2)}) async-start(), calls=%async_computation.14 | async-start | bytes 3932160 | tf_op jit(solution)/shard_map/reduce_scatter | solution.py:273
  354.9 11.6 all-to-all-start.7
  359.0 61.4 %reduce-scatter.11.cloned.1.call-start = ((), (), s32[]{:S(2)}) async-start(), calls=%async_computation.15 | async-start | bytes 3932160 | tf_op jit(solution)/shard_map/reduce_scatter | solution.py:273
  382.5 304.8 %all-reduce.10.cloned.1.call-start = ((), (), s32[]{:S(2)}) async-start(), calls=%async_computation.22 | async-start | bytes 37748736
  395.3 31.1 %copy-start.45 = (bf16[12,64,128]{2,1,0:T(8,128)(2,1)}, bf16[12,64,128]{2,1,0:T(8,128)(2,1)S(1)}, u32[]{:S(2)}) copy-start(bf16[12,64,128]{2,1,0:T(8,128)(2,1)S(1)} %fusion.87) | copy-start | bytes 589828
  464.1 507.8 %reduce-scatter.15.cloned.1.call-start = ((), (), s32[]{:S(2)}) async-start(), calls=%async_computation.17 | async-start | bytes 19464192 | tf_op jit(solution)/shard_map/reduce_scatter | solution.py:303
  478.1 776.5 %reduce-scatter.13.cloned.1.call-start = ((), (), s32[]{:S(2)}) async-start(), calls=%async_computation.16 | async-start | bytes 19464192 | tf_op jit(solution)/shard_map/reduce_scatter | solution.py:302
  503.6 73.8 %copy-start.17 = (f32[128,768]{1,0:T(8,128)S(1)}, f32[128,768]{1,0:T(8,128)}, u32[]{:S(2)}) copy-start(f32[128,768]{1,0:T(8,128)} %copy-done.15) | copy-start | bytes 1179652
  503.6 73.8 %copy-start.74 = (f32[128]{0:T(128)S(1)}, f32[128]{0:T(128)}, u32[]{:S(2)}) copy-start(f32[128]{0:T(128)} %get-tuple-element.88) | copy-start | bytes 1540
  (82 other events, 384.6 us)
Sparse Core Ops, SparseCore 0:
  10.2 43.1 all-gather.14
  57.0 26.0 all-gather.10
  85.3 22.5 all-gather.16
  109.4 47.5 all-gather.18
  161.5 25.7 all-gather.12
  188.8 22.5 all-gather.20
  291.0 37.7 reduce-scatter.8
  382.6 37.7 reduce-scatter.10
  464.3 222.9 all-reduce.9
  694.5 277.3 reduce-scatter.14
  978.3 276.3 reduce-scatter.12
where the time goes:
time: 1270 us; the launch traced here: 1260 us
  waiting for transfers between devices  860 us (68%)
  matrix products  137 us (11%)
  local copies, waits for them, and re-layouts  84.4 us (7%)
  blocking collectives  77.7 us (6%)
  other arithmetic  57 us (4%)
  starting transfers between devices  29.7 us (2%)
  between operations  15.5 us (1%)
    reduce_scatter x1, waiting for transfers between devices, on_device(): lax.psum_scatter(stacked(list_inner)[:, None], 'rep', scatter_dimension=2...  283 us
    reduce_scatter x1, waiting for transfers between devices, on_device(): lax.psum_scatter(stacked(list_outer)[:, None], 'rep', scatter_dimension=2...  282 us
    unnamed x12, waiting for transfers between devices  110 us
    unnamed x1, blocking collectives  67.7 us
    reduce_scatter x2, waiting for transfers between devices, on_device(): lax.psum_scatter(pair_grad, 'shard', scatter_dimension=0, tiled=True)  60 us
    all_gather x2, waiting for transfers between devices, on_device(): lax.all_gather(attn_in[level], 'shard', axis=0, tiled=True)  44.4 us
    another operation x8, local copies, waits for them, and re-layouts, stacked(): return jnp.stack(items[::-1], 0)  36.3 us
    all_gather x2, waiting for transfers between devices, on_device(): lax.all_gather(proj_qkv[:, model_width:], 'shard', axis=0, tiled=True)  33.5 us
  transfers between devices with their start and end apart: 18, of which 16 were waited for; matrix products, arithmetic and copies ran while one was open for 12% of the time, Pallas kernels for 0%

commit v1 on v0

v1 whole, which is shorter than its diff:
```python
import functools

import jax
import jax.numpy as jnp
from jax import lax
from jax.experimental import pallas as pl
from jax.experimental.pallas import tpu as pltpu
from jax.sharding import PartitionSpec as P

EPS = 1e-06
SCALE = 0.125
NEG = -1e30
THRESHOLDS = (12, 16, 23, 32, 46, 64, 91)
HIGH = lax.Precision.HIGHEST
F32 = jnp.float32
BF16 = jnp.bfloat16
BLK = 128
NX, NY, NZ = 4, 2, 4


def bucket_of(offset):
    distance = jnp.abs(offset)
    far_bucket = 8 + sum(((distance >= threshold).astype(jnp.int32) for threshold in THRESHOLDS))
    bucket_id = jnp.where(distance < 8, distance, far_bucket)
    return bucket_id + 16 * (offset > 0).astype(jnp.int32)


def rms_norm(vector, gain_vec):
    inverse = lax.rsqrt(jnp.mean(vector * vector, -1, keepdims=True) + EPS)
    return vector * inverse * gain_vec


def norm_back(vector, gain_vec, upstream):
    inverse = lax.rsqrt(jnp.mean(vector * vector, -1, keepdims=True) + EPS)
    scaled = upstream * gain_vec
    grad_gain = jnp.sum(upstream * vector * inverse, 0)
    grad_in = inverse * scaled - vector * (inverse * inverse * inverse) * jnp.mean(
        scaled * vector, -1, keepdims=True
    )
    return (grad_in, grad_gain)


def gelu_tanh(vector):
    return jax.nn.gelu(vector, approximate=True)


def dot(a, b, dims=((1,), (0,))):
    return lax.dot_general(a, b, (dims, ((), ())), preferred_element_type=F32)


def attn_fwd_kernel(q_ref, k_ref, v_ref, bias_ref, docq_ref, dock_ref, o_ref, p_ref):
    tok = q_ref.shape[0]
    nblk = tok // BLK
    first = lax.broadcasted_iota(jnp.int32, (1, BLK), 1) < BLK // 2
    k = k_ref[...]
    v = v_ref[...]
    for i in range(nblk):
        rows = slice(i * BLK, (i + 1) * BLK)
        same = docq_ref[rows, :] == dock_ref[...]
        q = q_ref[rows, :]
        outs = []
        for hh in range(2):
            mine = first if hh == 0 else jnp.logical_not(first)
            qm = jnp.where(mine, q, jnp.zeros_like(q))
            s = dot(qm, k, ((1,), (1,))) * SCALE
            bias = jnp.concatenate(
                [bias_ref[hh, max(-2, min(2, j - i)) + 2] for j in range(nblk)], axis=1
            )
            s = jnp.where(same, s + bias, NEG)
            e = jnp.exp(s - jnp.max(s, -1, keepdims=True))
            p = (e * (1.0 / jnp.sum(e, -1, keepdims=True))).astype(BF16)
            p_ref[hh, rows, :] = p
            outs.append(dot(p, v))
        o_ref[rows, :] = jnp.where(first, outs[0], outs[1]).astype(BF16)


def attn_fwd(qkv, bias, docq, dock):
    tok, width = qkv.shape
    heads_w = width // 3
    pairs = heads_w // BLK
    return pl.pallas_call(
        attn_fwd_kernel,
        grid=(pairs,),
        in_specs=[
            pl.BlockSpec((tok, BLK), lambda h: (0, h)),
            pl.BlockSpec((tok, BLK), lambda h: (0, pairs + h)),
            pl.BlockSpec((tok, BLK), lambda h: (0, 2 * pairs + h)),
            pl.BlockSpec((2, 5, BLK, BLK), lambda h: (h, 0, 0, 0)),
            pl.BlockSpec((tok, 1), lambda h: (0, 0)),
            pl.BlockSpec((1, tok), lambda h: (0, 0)),
        ],
        out_specs=[
            pl.BlockSpec((tok, BLK), lambda h: (0, h)),
            pl.BlockSpec((2, tok, tok), lambda h: (h, 0, 0)),
        ],
        out_shape=[
            jax.ShapeDtypeStruct((tok, heads_w), BF16),
            jax.ShapeDtypeStruct((2 * pairs, tok, tok), BF16),
        ],
        compiler_params=pltpu.CompilerParams(vmem_limit_bytes=40 * 1024 * 1024),
        cost_estimate=pl.CostEstimate(
            flops=8 * tok * tok * heads_w,
            bytes_accessed=8 * tok * width + 4 * pairs * tok * tok,
            transcendentals=2 * pairs * tok * tok,
        ),
        name="attn_fwd",
    )(qkv, qkv, qkv, bias, docq, dock)


def attn_bwd_kernel(q_ref, k_ref, v_ref, p_ref, do_ref, o_ref, dqkv_ref, m_ref, ds_ref):
    tok = q_ref.shape[0]
    nblk = tok // BLK
    pairs = pl.num_programs(0)
    step = pl.program_id(0)
    first = lax.broadcasted_iota(jnp.int32, (1, BLK), 1) < BLK // 2
    k = k_ref[...]
    v = v_ref[...]
    q = q_ref[...]
    do = do_ref[...]
    dk = jnp.zeros((tok, BLK), F32)
    dv = jnp.zeros((tok, BLK), F32)
    dqs = []
    for hh in range(2):
        mine = first if hh == 0 else jnp.logical_not(first)
        dom = jnp.where(mine, do, jnp.zeros_like(do))
        qm = jnp.where(mine, q, jnp.zeros_like(q))
        parts = [None] * 5
        dq_rows = []
        for i in range(nblk):
            rows = slice(i * BLK, (i + 1) * BLK)
            doi = dom[rows, :]
            dp = dot(doi, v, ((1,), (1,)))
            base = jnp.sum(
                doi.astype(F32) * o_ref[rows, :].astype(F32), -1, keepdims=True
            )
            ds = p_ref[hh, rows, :].astype(F32) * (dp - base)
            for j in range(nblk):
                d = max(-2, min(2, j - i)) + 2
                piece = ds[:, j * BLK : (j + 1) * BLK]
                parts[d] = piece if parts[d] is None else parts[d] + piece
            dsb = ds.astype(BF16)
            ds_ref[rows, :] = dsb
            dq_rows.append(dot(dsb, k))
        for d in range(5):
            m_ref[hh, d] = parts[d].astype(BF16)
        dqs.append(dq_rows)
        dk = dk + dot(ds_ref[...], qm, ((0,), (0,)))
        dv = dv + dot(p_ref[hh], dom, ((0,), (0,)))
    at = lambda part: pl.ds(pl.multiple_of((part * pairs + step) * BLK, BLK), BLK)
    for i in range(nblk):
        rows = slice(i * BLK, (i + 1) * BLK)
        dqkv_ref[rows, at(0)] = (jnp.where(first, dqs[0][i], dqs[1][i]) * SCALE).astype(BF16)
    dqkv_ref[:, at(1)] = (dk * SCALE).astype(BF16)
    dqkv_ref[:, at(2)] = dv.astype(BF16)


def attn_bwd(qkv, p, do, o):
    tok, width = qkv.shape
    heads_w = width // 3
    pairs = heads_w // BLK
    return pl.pallas_call(
        attn_bwd_kernel,
        grid=(pairs,),
        in_specs=[
            pl.BlockSpec((tok, BLK), lambda h: (0, h)),
            pl.BlockSpec((tok, BLK), lambda h: (0, pairs + h)),
            pl.BlockSpec((tok, BLK), lambda h: (0, 2 * pairs + h)),
            pl.BlockSpec((2, tok, tok), lambda h: (h, 0, 0)),
            pl.BlockSpec((tok, BLK), lambda h: (0, h)),
            pl.BlockSpec((tok, BLK), lambda h: (0, h)),
        ],
        out_specs=[
            pl.BlockSpec((tok, width), lambda h: (0, 0)),
            pl.BlockSpec((2, 5, BLK, BLK), lambda h: (h, 0, 0, 0)),
        ],
        out_shape=[
            jax.ShapeDtypeStruct((tok, width), BF16),
            jax.ShapeDtypeStruct((2 * pairs, 5, BLK, BLK), BF16),
        ],
        scratch_shapes=[pltpu.VMEM((tok, tok), BF16)],
        compiler_params=pltpu.CompilerParams(vmem_limit_bytes=40 * 1024 * 1024),
        cost_estimate=pl.CostEstimate(
            flops=20 * tok * tok * heads_w,
            bytes_accessed=12 * tok * width + 4 * pairs * tok * tok,
            transcendentals=0,
        ),
        name="attn_bwd",
    )(qkv, qkv, qkv, p, do, o)


def rep_index(x, yh, z):
    return ((x % NX) * NY + yh % NY) * NZ + z % NZ


def rep_shift(dx, dy, dz):
    return [
        (rep_index(x, y, z), rep_index(x + dx, y + dy, z + dz))
        for x in range(NX)
        for y in range(NY)
        for z in range(NZ)
    ]


def y_shift(dy, flip):
    reps = NX * NY * NZ
    pairs = []
    for x in range(NX):
        for yh in range(NY):
            for z in range(NZ):
                for yl in range(2):
                    for core in range(2):
                        y = (yh * 2 + yl + dy) % 4
                        source = (yl * 2 + core) * reps + rep_index(x, yh, z)
                        target = ((y % 2) * 2 + (core ^ flip)) * reps + rep_index(x, y // 2, z)
                        pairs.append((source, target))
    return pairs


def swap(value, bits):
    return lax.ppermute(value, "shard", [(s, s ^ bits) for s in range(4)])


def along_y(value, dy, flip):
    return lax.ppermute(value, ("shard", "rep"), y_shift(dy, flip))


def spread(value):
    near = swap(value, 1)
    far = swap(value, 2)
    return (value, near, far, swap(far, 1))


def in_order(values, me):
    a, b, c, d = values
    odd = (me & 1) == 1
    a, b = jnp.where(odd, b, a), jnp.where(odd, a, b)
    c, d = jnp.where(odd, d, c), jnp.where(odd, c, d)
    high = (me & 2) == 2
    return jnp.concatenate(
        [
            jnp.where(high, c, a),
            jnp.where(high, d, b),
            jnp.where(high, a, c),
            jnp.where(high, b, d),
        ],
        0,
    )


def take(array, index):
    return lax.dynamic_index_in_dim(array, index, 0, keepdims=False)


def exchange_sum(array, here, size, shift):
    total = take(array, here).astype(F32)
    for step in range(1, size):
        sent = take(array, (here + step) % size)
        total = total + lax.ppermute(sent, "rep", shift(step)).astype(F32)
    return total


def x_sum(array, x):
    return exchange_sum(array, x, NX, lambda s: rep_shift(s, 0, 0))


def z_sum(array, z):
    return exchange_sum(array, z, NZ, lambda s: rep_shift(0, 0, s))


def y_sum(array, y):
    return exchange_sum(array, y, NY, lambda s: rep_shift(0, s, 0))


def scatter_xzy(array, place):
    x, y, z = place
    rest = array.shape[1:]
    part = x_sum(array.reshape((NX, NY, NZ) + rest), x).astype(BF16)
    part = z_sum(jnp.swapaxes(part, 0, 1), z).astype(BF16)
    return y_sum(part, y)


def scatter_zxy(array, place):
    x, y, z = place
    rest = array.shape[1:]
    part = array.reshape((NX, NY, NZ) + rest)
    part = z_sum(jnp.moveaxis(part, 2, 0), z).astype(BF16)
    part = x_sum(part, x).astype(BF16)
    return y_sum(part, y)


def on_device(
    tokens,
    lengths,
    routes,
    attn_in,
    attn_proj,
    norm_first,
    norm_second,
    rel_bias,
    router,
    expert_in,
    expert_out,
    cotangent,
):
    me = lax.axis_index("shard")
    rep = lax.axis_index("rep")
    place = (rep // (NY * NZ), (rep // NZ) % NY, rep % NZ)
    core = me & 1
    odd = core == 1
    levels, own_rows, width3 = attn_in.shape
    width = width3 // 3
    half = width // 2
    tok = 4 * BLK
    heads = rel_bias.shape[2]
    heads_own = heads // 2
    buckets = rel_bias.shape[1]
    experts = router.shape[2]
    cap = BLK // 2

    def column_halves(block):
        parts = [block[..., i * half : (i + 1) * half] for i in range(6)]
        low = jnp.concatenate(parts[0::2], -1)
        high = jnp.concatenate(parts[1::2], -1)
        return jnp.where(odd, high, low), jnp.where(odd, low, high)

    mine, others = column_halves(attn_in)
    cut = own_rows // 2

    def gather_qkv(level, mine, others):
        near = swap(others, 1)
        same = jnp.concatenate(
            [along_y(mine[:cut], 1, 0), along_y(mine[cut:], -1, 0)], 0
        )
        cross = jnp.concatenate(
            [along_y(others[:cut], 1, 1), along_y(others[cut:], -1, 1)], 0
        )
        return in_order((mine, near, same, cross), me)

    token_parts = spread(tokens[0])
    route_parts = (routes[0], swap(routes[0], 1), swap(routes[0], 2), swap(routes[0], 3))
    w_qkv0 = gather_qkv(0, mine[0], others[0])
    x0 = in_order(token_parts, me)
    w_qkv0, x0, proj_own, mine1, others1, cot_own = lax.optimization_barrier(
        (w_qkv0, x0, attn_proj, mine[1], others[1], cotangent[0])
    )
    far = jnp.concatenate(
        [along_y(proj_own[:, :cut], 1, 0), along_y(proj_own[:, cut:], -1, 0)], 1
    )
    proj_parts = (proj_own, swap(proj_own, 1), far, swap(far, 1))
    w_proj = [in_order([part[level] for part in proj_parts], me) for level in range(levels)]
    w_qkv = [w_qkv0, gather_qkv(1, mine1, others1)]
    cot = in_order(spread(cot_own), me).astype(F32)

    position = jnp.arange(tok, dtype=jnp.int32)
    ends = jnp.cumsum(lengths[0])
    doc = jnp.sum((position[:, None] >= ends[None, :]).astype(jnp.int32), -1).astype(F32)
    docq, dock = doc[:, None], doc[None, :]
    offset = (
        BLK * (jnp.arange(5, dtype=jnp.int32) - 2)[:, None, None]
        + jnp.arange(BLK, dtype=jnp.int32)[None, None, :]
        - jnp.arange(BLK, dtype=jnp.int32)[None, :, None]
    )
    bucket_id = bucket_of(offset)
    bucket_hot = bucket_id[None] == jnp.arange(buckets, dtype=jnp.int32)[:, None, None, None]
    own_bias = jnp.where(odd, rel_bias[:, :, heads_own:], rel_bias[:, :, :heads_own])
    bias_blocks = jnp.einsum(
        "lbh,bdij->lhdij", own_bias, bucket_hot.astype(F32), precision=HIGH
    )
    route = in_order([part[None] for part in route_parts], me)
    onehot = (route[..., None] == jnp.arange(experts, dtype=jnp.int32)).astype(jnp.int32)
    slot = jnp.sum(jnp.cumsum(onehot, axis=1) * onehot, -1) - 1
    dispatch = (
        (route == me)[:, None, :] & (slot[:, None, :] == jnp.arange(cap)[None, :, None])
    ).astype(BF16)
    at_slot = jnp.arange(4, dtype=jnp.int32)[:, None] * cap + slot
    collect = [
        (
            (route.reshape(tok) == (me ^ r))[:, None]
            & (at_slot.reshape(tok)[:, None] == jnp.arange(4 * cap)[None, :])
        ).astype(BF16)
        for r in range(4)
    ]
    chosen = onehot.reshape(tok, experts).astype(F32)

    def rows_of(stream):
        return jnp.einsum(
            "bct,btd->bcd", dispatch, stream.reshape(4, BLK, -1), preferred_element_type=F32
        ).reshape(4 * cap, -1)

    def gathered(parts):
        return (
            dot(collect[0], parts[0])
            + dot(collect[1], parts[1])
            + dot(collect[2], parts[2])
            + dot(collect[3], parts[3])
        )

    def cols_of(array):
        return lax.dynamic_slice_in_dim(array, me * own_rows, own_rows, 1)

    saved = []
    stream = x0.astype(F32)
    for level in range(levels):
        normed = rms_norm(stream, norm_first[level]).astype(BF16)
        qkv = dot(normed, w_qkv[level]).astype(BF16)
        o_own, probs = attn_fwd(qkv, bias_blocks[level], docq, dock)
        o_near = swap(o_own, 1)
        mixed = jnp.concatenate(
            [jnp.where(odd, o_near, o_own), jnp.where(odd, o_own, o_near)], 1
        )
        after = stream + dot(mixed, w_proj[level])
        normed_two = rms_norm(after, norm_second[level]).astype(BF16)
        logits = dot(normed_two, router[level])
        route_probs = jax.nn.softmax(logits, -1)
        gate = jnp.sum(route_probs * chosen, -1)
        rows = rows_of(normed_two).astype(BF16)
        hidden = dot(rows, expert_in[level, 0])
        active = gelu_tanh(hidden).astype(BF16)
        made = dot(active, expert_out[level, 0]).astype(BF16)
        saved.append(
            (stream, normed, qkv, o_own, probs, mixed, after, normed_two, route_probs, gate,
             rows, hidden, active, made)
        )
        if level < levels - 1:
            stream = after + gate[:, None] * gathered(spread(made))

    blocks = made.reshape(4, cap, width)
    home = [take(blocks, me)] + [swap(take(blocks, me ^ r), r) for r in (1, 2, 3)]
    own_route, own_slot = take(route, me), take(slot, me)
    back = sum(
        dot(
            (
                (own_route == (me ^ r))[:, None]
                & (own_slot[:, None] == jnp.arange(cap)[None, :])
            ).astype(BF16),
            home[r],
        )
        for r in range(4)
    )
    own_gate = lax.dynamic_slice_in_dim(gate, me * BLK, BLK, 0)
    own_after = lax.dynamic_slice_in_dim(after, me * BLK, BLK, 0)
    result = (own_after + own_gate[:, None] * back).astype(BF16)[None]

    upstream = cot
    packs = [None] * levels
    inner_parts = [None] * levels
    outer_parts = [None] * levels
    for level in reversed(range(levels)):
        (stream, normed, qkv, o_own, probs, mixed, after, normed_two, route_probs, gate,
         rows, hidden, active, made) = saved[level]
        w_inner, w_outer = expert_in[level, 0], expert_out[level, 0]
        made_grad = rows_of((gate[:, None] * upstream).astype(BF16)).astype(BF16)
        active_grad = dot(made_grad, w_outer, ((1,), (1,)))
        _, gelu_pull = jax.vjp(gelu_tanh, hidden)
        hidden_grad = gelu_pull(active_grad)[0].astype(BF16)
        gate_grad = jnp.sum(made_grad.astype(F32) * made.astype(F32), -1)
        slot_probs = jnp.einsum(
            "bct,bte->bce", dispatch.astype(F32), route_probs.reshape(4, BLK, experts),
            precision=HIGH,
        ).reshape(4 * cap, experts)
        is_me = (jnp.arange(experts) == me).astype(F32)
        slot_logit_grad = gate_grad[:, None] * (is_me[None] - slot_probs)
        rows_grad = (
            dot(hidden_grad, w_inner, ((1,), (1,)))
            + dot(slot_logit_grad, router[level].astype(F32), ((1,), (1,)))
        ).astype(BF16)
        grads_home = spread(rows_grad)
        gate_home = (gate_grad, swap(gate_grad, 1), swap(gate_grad, 2), swap(gate_grad, 3))
        outer = dot(active, made_grad, ((0,), (0,))).astype(BF16)
        inner = dot(rows, hidden_grad, ((0,), (0,))).astype(BF16)
        inner_parts[level] = scatter_xzy(inner.reshape(32, width // 32, -1), place)
        outer_parts[level] = scatter_zxy(outer.reshape(32, outer.shape[0] // 32, -1), place)

        normed_grad = gathered(grads_home)
        token_gate_grad = sum(
            jnp.sum(collect[r].astype(F32) * gate_home[r][None], -1) for r in range(4)
        )
        logit_grad = token_gate_grad[:, None] * (chosen - route_probs)
        attn_side, grad_second = norm_back(after, norm_second[level], normed_grad)
        after_grad = upstream + attn_side
        branch_grad = after_grad.astype(BF16)
        w_proj_own = lax.dynamic_slice_in_dim(w_proj[level], core * half, half, 0)
        mixed_grad = dot(branch_grad, w_proj_own, ((1,), (1,))).astype(BF16)
        qkv_grad, bias_sums = attn_bwd(qkv, probs, mixed_grad, o_own)
        first_part = dot(qkv_grad, w_qkv[level], ((1,), (1,))).astype(BF16)
        first_grad = first_part.astype(F32) + swap(first_part, 1).astype(F32)
        input_side, grad_first = norm_back(stream, norm_first[level], first_grad)
        upstream = after_grad + input_side

        grad_proj = dot(cols_of(mixed), branch_grad, ((0,), (0,)))
        near_cols = lax.dynamic_slice_in_dim(normed, (me ^ 1) * own_rows, own_rows, 1)
        grad_qkv_own = dot(cols_of(normed), qkv_grad, ((0,), (0,))).astype(BF16)
        grad_qkv_near = swap(dot(near_cols, qkv_grad, ((0,), (0,))).astype(BF16), 1)
        pieces = []
        for part in range(3):
            a = grad_qkv_own[:, part * half : (part + 1) * half]
            b = grad_qkv_near[:, part * half : (part + 1) * half]
            pieces += [jnp.where(odd, b, a), jnp.where(odd, a, b)]
        bias_own = jnp.einsum(
            "hdij,bdij->bh", bias_sums, bucket_hot.astype(BF16), preferred_element_type=F32
        )
        bias_near = swap(bias_own, 1)
        grad_bias = jnp.concatenate(
            [jnp.where(odd, bias_near, bias_own), jnp.where(odd, bias_own, bias_near)], 1
        )
        grad_bias = lax.dynamic_slice_in_dim(
            grad_bias.reshape(-1), me * (buckets * heads // 4), buckets * heads // 4, 0
        )
        grad_router = dot(
            cols_of(normed_two).astype(F32), logit_grad, ((0,), (0,))
        )
        own_vec = lambda vec: lax.dynamic_slice_in_dim(vec, me * own_rows, own_rows, 0)
        small = jnp.concatenate(
            [
                own_vec(grad_first).reshape(32, -1),
                own_vec(grad_second).reshape(32, -1),
                grad_bias.reshape(32, -1),
                grad_router.reshape(32, -1),
            ],
            1,
        )
        small = jnp.pad(small, ((0, 0), (0, BLK - small.shape[1]))).astype(BF16)
        table = jnp.concatenate(pieces + [grad_proj.astype(BF16)], 1)
        packs[level] = (table.reshape(32, own_rows // 32, -1), small)

    per = own_rows // 32
    outs = []
    for level in range(levels):
        table, small = packs[level]
        flat = jnp.concatenate([table.reshape(32, -1), small], 1)
        summed = scatter_xzy(flat, place)
        big = summed[: per * 4 * width].reshape(per, 4 * width)
        tiny = summed[per * 4 * width :]
        outs.append(
            (
                big[:, :width3],
                big[:, width3:],
                tiny[:per],
                tiny[per : 2 * per],
                tiny[2 * per : 2 * per + buckets * heads // 128],
                tiny[2 * per + buckets * heads // 128 :][: per * experts].reshape(per, experts),
            )
        )
    stacked = [jnp.stack(items, 0) for items in zip(*outs)]
    expert_in_grad = jnp.stack(inner_parts, 0)[:, None]
    expert_out_grad = jnp.stack(outer_parts, 0)[:, None]
    own_up = lax.dynamic_slice_in_dim(upstream, me * BLK, BLK, 0)
    tokens_grad = own_up.astype(BF16)[None]
    return (result, tokens_grad, *stacked, expert_in_grad, expert_out_grad)


def solution(mesh):
    return jax.shard_map(
        on_device,
        mesh=mesh,
        in_specs=(
            P("rep", "shard", None),
            P("rep", None),
            P("rep", "shard"),
            P(None, "shard", None),
            P(None, "shard", None),
            P(),
            P(),
            P(),
            P(),
            P(None, "shard", None, None),
            P(None, "shard", None, None),
            P("rep", "shard", None),
        ),
        out_specs=(
            P("rep", "shard", None),
            P("rep", "shard", None),
            P(None, ("shard", "rep"), None),
            P(None, ("shard", "rep"), None),
            P(None, ("shard", "rep")),
            P(None, ("shard", "rep")),
            P(None, ("shard", "rep")),
            P(None, ("shard", "rep"), None),
            P(None, "shard", "rep", None),
            P(None, "shard", "rep", None),
        ),
        check_vma=False,
    )
```

time: 1270 us -> 547 us (0.43)
  waiting for transfers between devices: 860 us -> 151 us
  starting transfers between devices: 29.7 us -> 108 us
  blocking collectives: 77.7 us -> 0 us
  matrix products: 137 us -> 98.5 us
  Pallas kernels: 0 us -> 32.7 us
    reduce_scatter x4 -> x0, waiting for transfers between devices: 624 us -> none  [the longest x1 283 us: on_device(): lax.psum_scatter(stacked(list_inner)[:, None], 'rep', scatter_dimension=2...]
    ppermute x0 -> x91, waiting for transfers between devices: none -> 151 us  [the longest x42 119 us: exchange_sum(): total = total + lax.ppermute(sent, 'rep', shift(step)).astype(F32)]
    unnamed x12 -> x0, waiting for transfers between devices: 110 us -> none
    ppermute x0 -> x91, starting transfers between devices: none -> 108 us  [the longest x42 74.6 us: exchange_sum(): total = total + lax.ppermute(sent, 'rep', shift(step)).astype(F32)]
    all_gather x6 -> x0, waiting for transfers between devices: 98.1 us -> none  [the longest x2 44.4 us: on_device(): lax.all_gather(attn_in[level], 'shard', axis=0, tiled=True)]
    unnamed x1 -> x0, blocking collectives: 67.7 us -> none
    dot_general x54 -> x57, matrix products: 137 us -> 98.5 us  [the longest x48 82.7 us: dot(): return lax.dot_general(a, b, (dims, ((), ())), preferred_element_type=F32)]
    pallas_call x0 -> x4, Pallas kernels: none -> 32.7 us  [the longest x2 18.6 us: attn_fwd(): pl.pallas_call(attn_fwd_kernel, grid=(pairs,), in_specs=[pl.BlockSpec((to...]
  transfers between devices with their start and end apart: 18 -> 91, of which waited for: 16 -> 31; matrix products, arithmetic and copies ran while one was open for 12% -> 36% of each run, Pallas kernels for 0% -> 4%
where the time goes in v1:
time: 547 us; the launch traced here: 538 us
  waiting for transfers between devices  151 us (28%)
  starting transfers between devices  108 us (20%)
  matrix products  98.5 us (18%)
  local copies, waits for them, and re-layouts  80.8 us (15%)
  other arithmetic  63.3 us (12%)
  Pallas kernels  32.7 us (6%)
    ppermute x42, waiting for transfers between devices, exchange_sum(): total = total + lax.ppermute(sent, 'rep', shift(step)).astype(F32)  119 us
    dot_general x48, matrix products, dot(): return lax.dot_general(a, b, (dims, ((), ())), preferred_element_type=F32)  82.7 us
    ppermute x42, starting transfers between devices, exchange_sum(): total = total + lax.ppermute(sent, 'rep', shift(step)).astype(F32)  74.6 us
    ppermute x39, waiting for transfers between devices, swap(): return lax.ppermute(value, 'shard', [(s, s ^ bits) for s in range(4)])  20.7 us
    ppermute x39, starting transfers between devices, swap(): return lax.ppermute(value, 'shard', [(s, s ^ bits) for s in range(4)])  19 us
    unnamed x340, local copies, waits for them, and re-layouts  18.8 us
    pallas_call x2, Pallas kernels, attn_fwd(): pl.pallas_call(attn_fwd_kernel, grid=(pairs,), in_specs=[pl.BlockSpec((to...  18.6 us
    squeeze x15, local copies, waits for them, and re-layouts, take(): return lax.dynamic_index_in_dim(array, index, 0, keepdims=False)  14.7 us
  transfers between devices with their start and end apart: 91, of which 31 were waited for; matrix products, arithmetic and copies ran while one was open for 36% of the time, Pallas kernels for 4%

profile of v1, /device:TPU:0, one launch (start us, length us, event | category | flops | bytes accessed | tf_op | source)
XLA Modules:
  0.0 537.5 jit_solution(2226014976739976310)
XLA Ops:
  11.8 4.1 fusion.3
  19.0 4.5 copy_bitcast_fusion
  54.4 9.3 %attn_fwd.2 = (bf16[512,384]{1,0:T(8,128)(2,1)S(1)}, bf16[6,512,512]{2,1,0:T(8,128)(2,1)S(1)}) custom-call(bf16[512,1152]{1,0:T(8,128)(2,1)S(1)} %convolution_convert_fusion.5.q_ref.k_ref.v_ref, bf16[512,1152]{1,0:T(8,128)(2,1)S(1)} %convolution_convert_fusion.5.q_ref.k_ref.v_ref, bf16[512,1152]{1,0:T(8,128)(2,1)S(1)} %convolution_convert_fusion.5.q_ref.k_ref.v_ref, ...), custom_call_target="tpu_custom_call" | custom-call | flops 805306368 | bytes 7864320 | tf_op jit(solution)/shard_map/attn_fwd/pallas_call | solution.py:81
  67.5 7.1 %collective-permute-done.9 = bf16[2,96,768]{2,1,0:T(8,128)(2,1)S(1)} collective-permute-done((bf16[2,96,768]{2,1,0:T(8,128)(2,1)S(1)}, bf16[2,96,768]{2,1,0:T(8,128)(2,1)S(1)}, u32[]{:S(2)}, u32[]{:S(2)}) %collective-permute-start.9) | collective-permute-done | bytes 294944 | tf_op jit(solution)/shard_map/ppermute | solution.py:224
  84.9 3.9 fusion.22
  93.3 9.2 %collective-permute-done.17 = bf16[256,768]{1,0:T(8,128)(2,1)S(1)} collective-permute-done((bf16[256,768]{1,0:T(8,128)(2,1)S(1)}, bf16[256,768]{1,0:T(8,128)(2,1)S(1)}, u32[]{:S(2)}, u32[]{:S(2)}) %collective-permute-start.17) | collective-permute-done | bytes 393248 | tf_op jit(solution)/shard_map/ppermute | solution.py:220
  107.7 9.3 %attn_fwd.3 = (bf16[512,384]{1,0:T(8,128)(2,1)S(1)}, bf16[6,512,512]{2,1,0:T(8,128)(2,1)S(1)}) custom-call(bf16[512,1152]{1,0:T(8,128)(2,1)S(1)} %convolution_convert_fusion.4.q_ref.k_ref.v_ref, bf16[512,1152]{1,0:T(8,128)(2,1)S(1)} %convolution_convert_fusion.4.q_ref.k_ref.v_ref, bf16[512,1152]{1,0:T(8,128)(2,1)S(1)} %convolution_convert_fusion.4.q_ref.k_ref.v_ref, ...), custom_call_target="tpu_custom_call" | custom-call | flops 805306368 | bytes 7864320 | tf_op jit(solution)/shard_map/attn_fwd/pallas_call | solution.py:81
  134.0 6.0 %fusion.45 = bf16[256,3072]{1,0:T(8,128)(2,1)S(1)} fusion(f32[256,3072]{1,0:T(8,128)} %copy-done.151, bf16[256,768]{1,0:T(8,128)(2,1)S(1)} %bitcast.439, bf16[2,1,3072,768]{3,2,1,0:T(8,128)(2,1)} %param.22), kind=kOutput, calls=%fused_computation.53 | convolution fusion | flops 1223688192 | bytes 9830400 | tf_op jit(solution)/shard_map/dot_general | solution.py:48
  140.0 3.9 fusion.12
  182.4 7.1 %attn_bwd.2 = (bf16[512,1152]{1,0:T(8,128)(2,1)S(1)}, bf16[6,5,128,128]{3,2,1,0:T(8,128)(2,1)S(1)}) custom-call(bf16[512,1152]{1,0:T(8,128)(2,1)S(1)} %convolution_convert_fusion.4.q_ref.k_ref.v_ref, bf16[512,1152]{1,0:T(8,128)(2,1)S(1)} %convolution_convert_fusion.4.q_ref.k_ref.v_ref, bf16[512,1152]{1,0:T(8,128)(2,1)S(1)} %convolution_convert_fusion.4.q_ref.k_ref.v_ref, ...), custom_call_target="tpu_custom_call" | custom-call | flops 2013265920 | bytes 10223616 | tf_op jit(solution)/shard_map/attn_bwd/pallas_call | solution.py:161
  204.4 5.1 collective-permute-done.85
  215.7 16.7 %collective-permute-done.71 = bf16[2,4,24,3072]{3,2,0,1:T(8,128)(2,1)S(1)} collective-permute-done((bf16[2,4,24,3072]{3,2,0,1:T(8,128)(2,1)}, bf16[2,4,24,3072]{3,2,0,1:T(8,128)(2,1)S(1)}, u32[]{:S(2)}, u32[]{:S(2)}) %collective-permute-start.71) | collective-permute-done | bytes 1179680 | tf_op jit(solution)/shard_map/ppermute | solution.py:258
  232.5 17.6 %collective-permute-done.72 = bf16[2,4,24,3072]{3,2,0,1:T(8,128)(2,1)} collective-permute-done((bf16[2,4,24,3072]{3,2,0,1:T(8,128)(2,1)}, bf16[2,4,24,3072]{3,2,0,1:T(8,128)(2,1)}, u32[]{:S(2)}, u32[]{:S(2)}) %collective-permute-start.72) | collective-permute-done | bytes 1179680 | tf_op jit(solution)/shard_map/ppermute | solution.py:258
  276.2 9.3 %collective-permute-done.73 = bf16[2,24,3072]{2,1,0:T(8,128)(2,1)S(1)} collective-permute-done((bf16[2,24,3072]{2,1,0:T(8,128)(2,1)S(1)}, bf16[2,24,3072]{2,1,0:T(8,128)(2,1)S(1)}, u32[]{:S(2)}, u32[]{:S(2)}) %collective-permute-start.73) | collective-permute-done | bytes 294944 | tf_op jit(solution)/shard_map/ppermute | solution.py:258
  294.0 4.7 convolution_convert_fusion.1
  310.4 4.1 constant_dynamic-slice_fusion.7
  320.4 3.9 dynamic-slice_bitcast_fusion.5
  346.7 11.1 %collective-permute-done.56 = bf16[2,4,18560]{2,0,1:T(2,128)(2,1)S(1)} collective-permute-done((bf16[2,4,18560]{2,0,1:T(2,128)(2,1)}, bf16[2,4,18560]{2,0,1:T(2,128)(2,1)S(1)}, u32[]{:S(2)}, u32[]{:S(2)}) %collective-permute-start.56) | collective-permute-done | bytes 296992 | tf_op jit(solution)/shard_map/ppermute | solution.py:258
  391.2 7.1 %attn_bwd.3 = (bf16[512,1152]{1,0:T(8,128)(2,1)S(1)}, bf16[6,5,128,128]{3,2,1,0:T(8,128)(2,1)S(1)}) custom-call(bf16[512,1152]{1,0:T(8,128)(2,1)S(1)} %convolution_convert_fusion.5.q_ref.k_ref.v_ref, bf16[512,1152]{1,0:T(8,128)(2,1)S(1)} %convolution_convert_fusion.5.q_ref.k_ref.v_ref, bf16[512,1152]{1,0:T(8,128)(2,1)S(1)} %convolution_convert_fusion.5.q_ref.k_ref.v_ref, ...), custom_call_target="tpu_custom_call" | custom-call | flops 2013265920 | bytes 10223616 | tf_op jit(solution)/shard_map/attn_bwd/pallas_call | solution.py:161
  404.9 12.8 %collective-permute-done.77 = bf16[4,2,96,768]{3,2,1,0:T(8,128)(2,1)} collective-permute-done((bf16[4,2,96,768]{3,2,1,0:T(8,128)(2,1)}, bf16[4,2,96,768]{3,2,1,0:T(8,128)(2,1)}, u32[]{:S(2)}, u32[]{:S(2)}) %collective-permute-start.77) | collective-permute-done | bytes 1179680 | tf_op jit(solution)/shard_map/ppermute | solution.py:258
  417.7 4.5 collective-permute-start.65
  434.6 22.4 %collective-permute-done.65 = bf16[2,4,24,3072]{3,2,0,1:T(8,128)(2,1)} collective-permute-done((bf16[2,4,24,3072]{3,2,0,1:T(8,128)(2,1)S(1)}, bf16[2,4,24,3072]{3,2,0,1:T(8,128)(2,1)}, u32[]{:S(2)}, u32[]{:S(2)}) %collective-permute-start.65) | collective-permute-done | bytes 1179680 | tf_op jit(solution)/shard_map/ppermute | solution.py:258
  485.6 6.2 %collective-permute-done.68 = bf16[2,24,3072]{2,1,0:T(8,128)(2,1)S(1)} collective-permute-done((bf16[2,24,3072]{2,1,0:T(8,128)(2,1)S(1)}, bf16[2,24,3072]{2,1,0:T(8,128)(2,1)S(1)}, u32[]{:S(2)}, u32[]{:S(2)}) %collective-permute-start.68) | collective-permute-done | bytes 294944 | tf_op jit(solution)/shard_map/ppermute | solution.py:258
  508.1 8.1 %collective-permute-done.44 = bf16[2,4,18560]{2,0,1:T(2,128)(2,1)S(1)} collective-permute-done((bf16[2,4,18560]{2,0,1:T(2,128)(2,1)S(1)}, bf16[2,4,18560]{2,0,1:T(2,128)(2,1)S(1)}, u32[]{:S(2)}, u32[]{:S(2)}) %collective-permute-start.44) | collective-permute-done | bytes 296992 | tf_op jit(solution)/shard_map/ppermute | solution.py:258
  (764 shorter events, 336.3 us)
Async XLA Ops:
  2.4 38.5 %collective-permute-start.7 = (bf16[128,768]{1,0:T(8,128)(2,1)}, bf16[128,768]{1,0:T(8,128)(2,1)}, u32[]{:S(2)}, u32[]{:S(2)}) collective-permute-start(bf16[128,768]{1,0:T(8,128)(2,1)} %bitcast.442), channel_id=1, source_target_pairs={{0,32},{32,0},{64,96},{96,64},{1,33},{33,1},{65,97},{97,65},{2,34}... | collective-permute-start | bytes 589832 | tf_op jit(solution)/shard_map/ppermute | solution.py:220
  43.4 36.2 %collective-permute-start.23 = (bf16[192,1152]{1,0:T(8,128)(2,1)S(1)}, bf16[192,1152]{1,0:T(8,128)(2,1)S(1)}, u32[]{:S(2)}, u32[]{:S(2)}) collective-permute-start(bf16[192,1152]{1,0:T(8,128)(2,1)S(1)} %copy-done.53), channel_id=1, source_target_pairs={{0,32},{32,0},{64,96},{96,64},{1,33},{33,1},{65,97},{97,65},{2,34}... | collective-permute-start | bytes 1327112 | tf_op jit(solution)/shard_map/ppermute | solution.py:220
  152.6 45.8 %collective-permute-start.84 = (bf16[4,2,96,768]{3,2,1,0:T(8,128)(2,1)}, bf16[4,2,96,768]{3,2,1,0:T(8,128)(2,1)}, u32[]{:S(2)}, u32[]{:S(2)}) collective-permute-start(bf16[4,2,96,768]{3,2,1,0:T(8,128)(2,1)} %get-tuple-element.110), channel_id=1, source_target_pairs={{0,1},{1,2},{2,3},{3,0},{4,5},{5,6},{6,7},{7,4},{8,9},{9,10},{10,1... | collective-permute-start | bytes 3538952 | tf_op jit(solution)/shard_map/ppermute | solution.py:258
  154.5 55.0 %collective-permute-start.85 = (bf16[4,2,96,768]{3,2,1,0:T(8,128)(2,1)}, bf16[4,2,96,768]{3,2,1,0:T(8,128)(2,1)}, u32[]{:S(2)}, u32[]{:S(2)}) collective-permute-start(bf16[4,2,96,768]{3,2,1,0:T(8,128)(2,1)} %get-tuple-element.112), channel_id=1, source_target_pairs={{0,2},{1,3},{2,0},{3,1},{4,6},{5,7},{6,4},{7,5},{8,10},{9,11},{10,... | collective-permute-start | bytes 3538952 | tf_op jit(solution)/shard_map/ppermute | solution.py:258
  173.5 36.1 %collective-permute-start.86 = (bf16[4,2,96,768]{3,2,1,0:T(8,128)(2,1)}, bf16[4,2,96,768]{3,2,1,0:T(8,128)(2,1)}, u32[]{:S(2)}, u32[]{:S(2)}) collective-permute-start(bf16[4,2,96,768]{3,2,1,0:T(8,128)(2,1)} %get-tuple-element.111), channel_id=1, source_target_pairs={{0,3},{1,0},{2,1},{3,2},{4,7},{5,4},{6,5},{7,6},{8,11},{9,8},{10,9... | collective-permute-start | bytes 3538952 | tf_op jit(solution)/shard_map/ppermute | solution.py:258
  175.9 39.2 %collective-permute-start.70 = (bf16[2,4,24,3072]{3,2,0,1:T(8,128)(2,1)}, bf16[2,4,24,3072]{3,2,0,1:T(8,128)(2,1)}, u32[]{:S(2)}, u32[]{:S(2)}) collective-permute-start(bf16[2,4,24,3072]{3,2,0,1:T(8,128)(2,1)} %bitcast.411), channel_id=1, source_target_pairs={{0,8},{1,9},{2,10},{3,11},{4,12},{5,13},{6,14},{7,15},{8,16},{9,17... | collective-permute-start | bytes 3538952 | tf_op jit(solution)/shard_map/ppermute | solution.py:258
  195.7 36.8 %collective-permute-start.71 = (bf16[2,4,24,3072]{3,2,0,1:T(8,128)(2,1)}, bf16[2,4,24,3072]{3,2,0,1:T(8,128)(2,1)S(1)}, u32[]{:S(2)}, u32[]{:S(2)}) collective-permute-start(bf16[2,4,24,3072]{3,2,0,1:T(8,128)(2,1)} %bitcast.436), channel_id=1, source_target_pairs={{0,16},{1,17},{2,18},{3,19},{4,20},{5,21},{6,22},{7,23},{8,24},{9,... | collective-permute-start | bytes 3538952 | tf_op jit(solution)/shard_map/ppermute | solution.py:258
  198.4 51.6 %collective-permute-start.72 = (bf16[2,4,24,3072]{3,2,0,1:T(8,128)(2,1)}, bf16[2,4,24,3072]{3,2,0,1:T(8,128)(2,1)}, u32[]{:S(2)}, u32[]{:S(2)}) collective-permute-start(bf16[2,4,24,3072]{3,2,0,1:T(8,128)(2,1)} %bitcast.435), channel_id=1, source_target_pairs={{0,24},{1,25},{2,26},{3,27},{4,28},{5,29},{6,30},{7,31},{8,0},{9,1... | collective-permute-start | bytes 3538952 | tf_op jit(solution)/shard_map/ppermute | solution.py:258
  209.5 109.7 %collective-permute-start.53 = (f32[256]{0:T(256)}, f32[256]{0:T(256)}, u32[]{:S(2)}, u32[]{:S(2)}) collective-permute-start(f32[256]{0:T(256)} %get-tuple-element.234), channel_id=1, source_target_pairs={{0,32},{32,0},{64,96},{96,64},{1,33},{33,1},{65,97},{97,65},{2,34}... | collective-permute-start | bytes 3080 | tf_op jit(solution)/shard_map/ppermute | solution.py:220
  209.5 119.1 %collective-permute-start.54 = (f32[256]{0:T(256)}, f32[256]{0:T(256)}, u32[]{:S(2)}, u32[]{:S(2)}) collective-permute-start(f32[256]{0:T(256)} %get-tuple-element.234), channel_id=1, source_target_pairs={{0,64},{32,96},{64,0},{96,32},{1,65},{33,97},{65,1},{97,33},{2,66}... | collective-permute-start | bytes 3080 | tf_op jit(solution)/shard_map/ppermute | solution.py:220
  215.5 40.8 %collective-permute-start.51 = (bf16[192,1152]{1,0:T(8,128)(2,1)S(1)}, bf16[192,1152]{1,0:T(8,128)(2,1)S(1)}, u32[]{:S(2)}, u32[]{:S(2)}) collective-permute-start(bf16[192,1152]{1,0:T(8,128)(2,1)S(1)} %copy-done.80), channel_id=1, source_target_pairs={{0,32},{32,0},{64,96},{96,64},{1,33},{33,1},{65,97},{97,65},{2,34}... | collective-permute-start | bytes 1327112 | tf_op jit(solution)/shard_map/ppermute | solution.py:220
  232.5 37.8 %collective-permute-start.87 = (bf16[2,96,768]{2,1,0:T(8,128)(2,1)}, bf16[2,96,768]{2,1,0:T(8,128)(2,1)}, u32[]{:S(2)}, u32[]{:S(2)}) collective-permute-start(bf16[2,96,768]{2,1,0:T(8,128)(2,1)} %get-tuple-element.154), channel_id=1, source_target_pairs={{0,8},{1,9},{2,10},{3,11},{4,12},{5,13},{6,14},{7,15},{8,16},{9,17... | collective-permute-start | bytes 884744 | tf_op jit(solution)/shard_map/ppermute | solution.py:258
  285.5 45.8 %collective-permute-start.55 = (f32[256]{0:T(256)}, f32[256]{0:T(256)}, u32[]{:S(2)}, u32[]{:S(2)}) collective-permute-start(f32[256]{0:T(256)} %get-tuple-element.234), channel_id=1, source_target_pairs={{0,96},{32,64},{64,32},{96,0},{1,97},{33,65},{65,33},{97,1},{2,98}... | collective-permute-start | bytes 3080 | tf_op jit(solution)/shard_map/ppermute | solution.py:220
  332.2 37.7 %collective-permute-start.35 = (bf16[256,768]{1,0:T(8,128)(2,1)}, bf16[256,768]{1,0:T(8,128)(2,1)}, u32[]{:S(2)}, u32[]{:S(2)}) collective-permute-start(bf16[256,768]{1,0:T(8,128)(2,1)} %copy-done.57), channel_id=1, source_target_pairs={{0,32},{32,0},{64,96},{96,64},{1,33},{33,1},{65,97},{97,65},{2,34}... | collective-permute-start | bytes 1179656 | tf_op jit(solution)/shard_map/ppermute | solution.py:220
  365.2 52.5 %collective-permute-start.77 = (bf16[4,2,96,768]{3,2,1,0:T(8,128)(2,1)}, bf16[4,2,96,768]{3,2,1,0:T(8,128)(2,1)}, u32[]{:S(2)}, u32[]{:S(2)}) collective-permute-start(bf16[4,2,96,768]{3,2,1,0:T(8,128)(2,1)} %get-tuple-element.107), channel_id=1, source_target_pairs={{0,1},{1,2},{2,3},{3,0},{4,5},{5,6},{6,7},{7,4},{8,9},{9,10},{10,1... | collective-permute-start | bytes 3538952 | tf_op jit(solution)/shard_map/ppermute | solution.py:258
  366.1 60.8 %collective-permute-start.78 = (bf16[4,2,96,768]{3,2,1,0:T(8,128)(2,1)}, bf16[4,2,96,768]{3,2,1,0:T(8,128)(2,1)}, u32[]{:S(2)}, u32[]{:S(2)}) collective-permute-start(bf16[4,2,96,768]{3,2,1,0:T(8,128)(2,1)} %get-tuple-element.109), channel_id=1, source_target_pairs={{0,2},{1,3},{2,0},{3,1},{4,6},{5,7},{6,4},{7,5},{8,10},{9,11},{10,... | collective-permute-start | bytes 3538952 | tf_op jit(solution)/shard_map/ppermute | solution.py:258
  369.0 58.1 %collective-permute-start.79 = (bf16[4,2,96,768]{3,2,1,0:T(8,128)(2,1)}, bf16[4,2,96,768]{3,2,1,0:T(8,128)(2,1)}, u32[]{:S(2)}, u32[]{:S(2)}) collective-permute-start(bf16[4,2,96,768]{3,2,1,0:T(8,128)(2,1)} %get-tuple-element.108), channel_id=1, source_target_pairs={{0,3},{1,0},{2,1},{3,2},{4,7},{5,4},{6,5},{7,6},{8,11},{9,8},{10,9... | collective-permute-start | bytes 3538952 | tf_op jit(solution)/shard_map/ppermute | solution.py:258
  369.9 61.5 %collective-permute-start.63 = (bf16[2,4,24,3072]{3,2,0,1:T(8,128)(2,1)}, bf16[2,4,24,3072]{3,2,0,1:T(8,128)(2,1)}, u32[]{:S(2)}, u32[]{:S(2)}) collective-permute-start(bf16[2,4,24,3072]{3,2,0,1:T(8,128)(2,1)} %bitcast.414), channel_id=1, source_target_pairs={{0,8},{1,9},{2,10},{3,11},{4,12},{5,13},{6,14},{7,15},{8,16},{9,17... | collective-permute-start | bytes 3538952 | tf_op jit(solution)/shard_map/ppermute | solution.py:258
  417.7 39.2 %collective-permute-start.65 = (bf16[2,4,24,3072]{3,2,0,1:T(8,128)(2,1)S(1)}, bf16[2,4,24,3072]{3,2,0,1:T(8,128)(2,1)}, u32[]{:S(2)}, u32[]{:S(2)}) collective-permute-start(bf16[2,4,24,3072]{3,2,0,1:T(8,128)(2,1)S(1)} %bitcast.434), channel_id=1, source_target_pairs={{0,24},{1,25},{2,26},{3,27},{4,28},{5,29},{6,30},{7,31},{8,0},{9,1... | collective-permute-start | bytes 3538952 | tf_op jit(solution)/shard_map/ppermute | solution.py:258
  426.9 70.0 %collective-permute-start.38 = (bf16[512,768]{1,0:T(8,128)(2,1)}, bf16[512,768]{1,0:T(8,128)(2,1)}, u32[]{:S(2)}, u32[]{:S(2)}) collective-permute-start(bf16[512,768]{1,0:T(8,128)(2,1)} %convolution_convert_fusion.10), channel_id=1, source_target_pairs={{0,32},{32,0},{64,96},{96,64},{1,33},{33,1},{65,97},{97,65},{2,34}... | collective-permute-start | bytes 2359304 | tf_op jit(solution)/shard_map/ppermute | solution.py:220
  427.0 36.3 %collective-permute-start.39 = (bf16[192,1152]{1,0:T(8,128)(2,1)}, bf16[192,1152]{1,0:T(8,128)(2,1)S(1)}, u32[]{:S(2)}, u32[]{:S(2)}) collective-permute-start(bf16[192,1152]{1,0:T(8,128)(2,1)} %convolution_convert_fusion.9), channel_id=1, source_target_pairs={{0,32},{32,0},{64,96},{96,64},{1,33},{33,1},{65,97},{97,65},{2,34}... | collective-permute-start | bytes 1327112 | tf_op jit(solution)/shard_map/ppermute | solution.py:220
  431.4 44.8 %collective-permute-start.80 = (bf16[2,96,768]{2,1,0:T(8,128)(2,1)}, bf16[2,96,768]{2,1,0:T(8,128)(2,1)}, u32[]{:S(2)}, u32[]{:S(2)}) collective-permute-start(bf16[2,96,768]{2,1,0:T(8,128)(2,1)} %get-tuple-element.151), channel_id=1, source_target_pairs={{0,8},{1,9},{2,10},{3,11},{4,12},{5,13},{6,14},{7,15},{8,16},{9,17... | collective-permute-start | bytes 884744 | tf_op jit(solution)/shard_map/ppermute | solution.py:258
  431.8 45.9 %collective-permute-start.81 = (bf16[2,96,768]{2,1,0:T(8,128)(2,1)}, bf16[2,96,768]{2,1,0:T(8,128)(2,1)}, u32[]{:S(2)}, u32[]{:S(2)}) collective-permute-start(bf16[2,96,768]{2,1,0:T(8,128)(2,1)} %get-tuple-element.153), channel_id=1, source_target_pairs={{0,16},{1,17},{2,18},{3,19},{4,20},{5,21},{6,22},{7,23},{8,24},{9,... | collective-permute-start | bytes 884744 | tf_op jit(solution)/shard_map/ppermute | solution.py:258
  482.5 40.7 %collective-permute-start.83 = (bf16[96,768]{1,0:T(8,128)(2,1)}, bf16[96,768]{1,0:T(8,128)(2,1)}, u32[]{:S(2)}, u32[]{:S(2)}) collective-permute-start(bf16[96,768]{1,0:T(8,128)(2,1)} %dynamic-slice_bitcast_fusion.25), channel_id=1, source_target_pairs={{0,4},{1,5},{2,6},{3,7},{4,0},{5,1},{6,2},{7,3},{8,12},{9,13},{10,... | collective-permute-start | bytes 442376 | tf_op jit(solution)/shard_map/ppermute | solution.py:258
  (232 other events, 2694.1 us)
